TPU v7x, 32 devices: a whole 2x2x4 slice. The times are simulated.
32 devices in a mesh: dp: 4 (over y, x), tensor: 8 (over z, core).
Axes of the slice: x: 2, y: 2, z: 4, core: 2. Of those that a mesh axis runs over, the one named last changes fastest.
Arguments:
- tokens: bfloat16 [1024, 8192], P('dp'), may hold values from -6 to 6
- out_grad: bfloat16 [1024, 8192], P('dp'), may hold values from -6 to 6
- weight_tiles: bfloat16 [256, 2, 3, 128, 128], P(('dp', 'tensor')), may hold values from -0.125 to 0.125
- tile_places: int32 [256, 2], P(('dp', 'tensor')), may hold values from 0 to 1663, as said below
- live_counts: int32 [256], P(('dp', 'tensor')), may hold values from 0 to 2, as said below
Outputs:
- layer_out: bfloat16 [1024, 8192], P('dp', 'tensor')
- input_grad: bfloat16 [1024, 8192], P('dp', 'tensor')
Inputs may be any that keep to these rules, and one draw needn't show every extreme that they name: `tile_places`: among the slots addressed to one owner, live or not, no two have the same place; the place 64 * 26 - 1 occurs in a live slot of every owner. `live_counts`: every owner receives 2 live slots from some source, and some owner receives 2 live slots from every source; slots past the count hold padding.
All inputs are finite; a program needn't handle non-finite values.
Results may differ from a plain program's by a relative error of at most 0.012.
Values may be sent and summed in bfloat16 or wider, within the bound.
A program may use at most 192 MiB of HBM per device.

v0:
```python
import jax
import jax.numpy as jnp
from jax import lax
from jax.sharding import PartitionSpec as P

FF = 26624


def block_length(extent):
    length = min(extent, 32)
    while extent % length:
        length -= 1
    return length


def over_blocks(step, running, arrays):
    extent = arrays[0].shape[0]
    length = block_length(extent)
    shaped = tuple((item.reshape((extent // length, length) + item.shape[1:]) for item in arrays))

    def advance(acc_value, slot_block):
        return (step(acc_value, slot_block), None)

    running, _ = lax.scan(advance, running, shaped)
    return running


def body(tokens, out_grad, weight_tiles, tile_places, live_counts):
    tok_rows = tokens.shape[0]
    feat_width = tokens.shape[1]
    tile_side = weight_tiles.shape[-1]
    peer_slots = weight_tiles.shape[1]
    row_count = feat_width // tile_side
    owners = lax.axis_size("tensor")
    col_count = FF // (tile_side * owners)
    arrived_tiles, arrived_places, arrived_counts = (
        lax.all_to_all(weight_tiles, "tensor", split_axis=0, concat_axis=0, tiled=True),
        lax.all_to_all(tile_places, "tensor", split_axis=0, concat_axis=0, tiled=True),
        lax.all_to_all(live_counts, "tensor", split_axis=0, concat_axis=0, tiled=True),
    )
    slot_tiles, slot_places, slot_counts = (
        lax.all_gather(arrived_tiles, "dp", axis=0, tiled=True),
        lax.all_gather(arrived_places, "dp", axis=0, tiled=True),
        lax.all_gather(arrived_counts, "dp", axis=0, tiled=True),
    )
    slot_total = slot_places.shape[0] * peer_slots
    row_ids = (slot_places // col_count).reshape(-1).astype(jnp.int32)
    col_ids = (slot_places % col_count).reshape(-1).astype(jnp.int32)
    live_mask = (jnp.arange(peer_slots)[None, :] < slot_counts[:, None]).reshape(-1)
    flat_tiles = slot_tiles.reshape((slot_total,) + slot_tiles.shape[2:])
    flat_tiles = jnp.where(
        live_mask[:, None, None, None], flat_tiles, jnp.zeros((), flat_tiles.dtype)
    )
    slot_data = (flat_tiles, row_ids, col_ids)
    token_blocks = tokens.reshape(tok_rows, row_count, tile_side)

    def gate_up_step(acc_value, slot_block):
        weights, row_block, col_block = slot_block
        gathered = jnp.take(token_blocks, row_block, axis=1)
        products = jnp.einsum(
            "tsa,sgab->gtsb", gathered, weights[:, 0:2], preferred_element_type=jnp.float32
        )
        return acc_value.at[:, :, col_block, :].add(products)

    preact = over_blocks(
        gate_up_step, jnp.zeros((2, tok_rows, col_count, tile_side), jnp.float32), slot_data
    )
    gate_pre = preact[0]
    up_pre = preact[1]
    sigmoid_gate = jax.nn.sigmoid(gate_pre)
    gate_act = gate_pre * sigmoid_gate
    hidden = (gate_act * up_pre).astype(jnp.bfloat16)

    def down_step(acc_value, slot_block):
        weights, row_block, col_block = slot_block
        gathered = jnp.take(hidden, col_block, axis=1)
        products = jnp.einsum(
            "tsa,sab->tsb", gathered, weights[:, 2], preferred_element_type=jnp.float32
        )
        return acc_value.at[:, row_block, :].add(products)

    out_part = over_blocks(
        down_step, jnp.zeros((tok_rows, row_count, tile_side), jnp.float32), slot_data
    ).reshape(tok_rows, feat_width)
    layer_out = lax.psum_scatter(
        out_part.astype(jnp.bfloat16), "tensor", scatter_dimension=1, tiled=True
    )
    grad_blocks = out_grad.reshape(tok_rows, row_count, tile_side)

    def back_step(acc_value, slot_block):
        weights, row_block, col_block = slot_block
        gathered = jnp.take(grad_blocks, row_block, axis=1)
        products = jnp.einsum(
            "tsb,sab->tsa", gathered, weights[:, 2], preferred_element_type=jnp.float32
        )
        return acc_value.at[:, col_block, :].add(products)

    grad_hidden = over_blocks(
        back_step, jnp.zeros((tok_rows, col_count, tile_side), jnp.float32), slot_data
    )
    grad_gate = (
        grad_hidden * up_pre * (sigmoid_gate * (1.0 + gate_pre * (1.0 - sigmoid_gate)))
    ).astype(jnp.bfloat16)
    grad_up = (grad_hidden * gate_act).astype(jnp.bfloat16)
    grad_pair = jnp.stack([grad_gate, grad_up])

    def input_step(acc_value, slot_block):
        weights, row_block, col_block = slot_block
        gathered = jnp.take(grad_pair, col_block, axis=2)
        products = jnp.einsum(
            "gtsb,sgab->tsa", gathered, weights[:, 0:2], preferred_element_type=jnp.float32
        )
        return acc_value.at[:, row_block, :].add(products)

    in_part = over_blocks(
        input_step, jnp.zeros((tok_rows, row_count, tile_side), jnp.float32), slot_data
    ).reshape(tok_rows, feat_width)
    input_grad = lax.psum_scatter(
        in_part.astype(jnp.bfloat16), "tensor", scatter_dimension=1, tiled=True
    )
    return (layer_out, input_grad)


def solution(mesh):
    in_specs = (
        P("dp", None),
        P("dp", None),
        P(("dp", "tensor"), None, None, None, None),
        P(("dp", "tensor"), None),
        P(("dp", "tensor")),
    )
    out_specs = (P("dp", "tensor"), P("dp", "tensor"))
    return jax.shard_map(body, mesh=mesh, in_specs=in_specs, out_specs=out_specs, check_vma=False)
```

profile of v0, /device:TPU:0, one launch (start us, length us, event | category | flops | bytes accessed | tf_op | source)
XLA Modules:
  0.0 404.7 jit_solution(2578205139297796959)
XLA Ops:
  7.2 44.3 %all_to_all.29 = bf16[8,2,3,128,128]{4,3,2,1,0:T(8,128)(2,1)} all-to-all(bf16[8,2,3,128,128]{4,3,2,1,0:T(8,128)(2,1)} %param.17), channel_id=1, replica_groups=mesh['dp'=4,'tensor'=8] {'tensor'}, dimensions={0} | all-to-all | bytes 3145728 | tf_op jit(solution)/shard_map/all_to_all | solution.py:37
  52.2 3.3 all-to-all-start.1
  56.3 6.7 %copy.90 = bf16[256,8192]{0,1:T(8,128)(2,1)} copy(bf16[256,8192]{1,0:T(8,128)(2,1)} %param.16) | data formatting | bytes 8388608 | tf_op args[1]
  63.0 6.4 %copy.92 = bf16[256,64,128]{2,0,1:T(8,128)(2,1)} copy(bf16[256,64,128]{0,2,1:T(8,128)(2,1)} %bitcast.209) | data formatting | bytes 8388608 | tf_op jit(solution)/shard_map/while | solution.py:24
  69.4 6.4 %copy.85 = bf16[256,8192]{0,1:T(8,128)(2,1)} copy(bf16[256,8192]{1,0:T(8,128)(2,1)} %param.15) | data formatting | bytes 8388608 | tf_op args[0]
  75.8 6.4 %copy.87 = bf16[256,64,128]{2,0,1:T(8,128)(2,1)} copy(bf16[256,64,128]{0,2,1:T(8,128)(2,1)} %bitcast.210) | data formatting | bytes 8388608 | tf_op jit(solution)/shard_map/while | solution.py:24
  83.4 5.0 %all-to-all-start = ((s32[8,1,2]{2,1,0:T(1,128)}), s32[8,1,2]{2,1,0:T(1,128)S(1)}, u32[]{:S(2)}, u32[]{:S(2)}) async-start(s32[8,1,2]{2,1,0:T(1,128)} %copy.78), calls=%async_computation | async-start | bytes 8192 | tf_op jit(solution)/shard_map/all_to_all | solution.py:38
  88.9 7.5 %all-reduce = s32[32]{0:T(128)S(1)} all-reduce(s32[32]{0:T(128)S(1)} %dynamic-update-slice), channel_id=3, replica_groups=mesh['dp'=4,'tensor'=8] {'dp'}, use_global_device_ids=true, to_apply=%add | all-reduce | flops 32 | bytes 256
  96.7 8.3 %all-gather = s32[32,1,2]{2,1,0:T(1,128)S(1)} all-gather(s32[8,1,2]{2,1,0:T(1,128)S(1)} %all-to-all-done), channel_id=2, replica_groups=mesh['dp'=4,'tensor'=8] {'dp'}, dimensions={0}, use_global_device_ids=true | all-gather | bytes 320 | tf_op jit(solution)/shard_map/all_gather | solution.py:43
  105.5 15.5 %all-gather.4.cloned.1.call-done = bf16[32,2,3,128,128]{4,3,2,1,0:T(8,128)(2,1)} async-done(((bf16[8,2,3,128,128]{4,3,2,1,0:T(8,128)(2,1)}), bf16[32,2,3,128,128]{4,3,2,1,0:T(8,128)(2,1)}) %all-gather.4.cloned.1.call-update) | async-done | bytes 6291472 | tf_op jit(solution)/shard_map/all_gather | solution.py:42
  121.0 3.3 bitcast_select_fusion
  124.3 4.5 %copy.88 = bf16[2,32,3,128,128]{4,3,1,2,0:T(8,128)(2,1)} copy(bf16[2,32,3,128,128]{4,3,2,1,0:T(8,128)(2,1)S(1)} %bitcast_select_fusion) | data formatting | bytes 12582912 | tf_op jit(solution)/shard_map/while | solution.py:24
  129.2 32.5 %while.42 = (s32[]{:T(128)}, f32[256,26,128]{2,0,1:T(8,128)S(1)}, s32[2,32]{1,0:T(2,128)S(1)}, bf16[2,32,3,128,128]{4,3,1,2,0:T(8,128)(2,1)}, s32[2,32]{1,0:T(2,...) while((s32[]{:T(128)}, f32[256,26,128]{2,0,1:T(8,128)S(1)}, s32[2,32]{1,0:T(2,128)S(1)}, ...), condition=%wide.region_9.11_spmd, body=%wide.region_7.10_spmd.sunk | while | flops 270533920 | bytes 38802964 | solution.py:24
  129.4 4.3 %gather_fusion.2 = bf16[32,256,128]{2,1,0:T(8,128)(2,1)} fusion(bf16[256,64,128]{2,0,1:T(8,128)(2,1)} %get-tuple-element.508, s32[1024]{0:T(1024)S(1)} %pad_clamp_fusion.10), kind=kCustom, calls=%fused_computation.3.clone.clone.1 | custom fusion | bytes 4194432 | tf_op jit(solution)/shard_map/while/body/eval_jaxpr/jit(_take)/gather | solution.py:92
  136.3 2.7 fusion.74
  139.0 6.5 %scatter_fusion.2 = f32[256,26,128]{2,0,1:T(8,128)S(1)} fusion(f32[256,26,128]{2,0,1:T(8,128)S(1)} %get-tuple-element.497, s32[32]{0:T(128)S(1)} %fusion.73, f32[32,256,128]{2,1,0:T(8,128)} %fusion.74), kind=kCustom, calls=%fused_computation.7.clone.1 | custom fusion | flops 1048576 | bytes 12583040 | tf_op jit(solution)/shard_map/while/body/eval_jaxpr/scatter-add | solution.py:96
  145.5 4.3 %gather_fusion.2 = bf16[32,256,128]{2,1,0:T(8,128)(2,1)} fusion(bf16[256,64,128]{2,0,1:T(8,128)(2,1)} %get-tuple-element.508, s32[1024]{0:T(1024)S(1)} %pad_clamp_fusion.10), kind=kCustom, calls=%fused_computation.3.clone.clone.1 | custom fusion | bytes 4194432 | tf_op jit(solution)/shard_map/while/body/eval_jaxpr/jit(_take)/gather | solution.py:92
  152.4 2.7 fusion.74
  155.1 6.5 %scatter_fusion.2 = f32[256,26,128]{2,0,1:T(8,128)S(1)} fusion(f32[256,26,128]{2,0,1:T(8,128)S(1)} %get-tuple-element.497, s32[32]{0:T(128)S(1)} %fusion.73, f32[32,256,128]{2,1,0:T(8,128)} %fusion.74), kind=kCustom, calls=%fused_computation.7.clone.1 | custom fusion | flops 1048576 | bytes 12583040 | tf_op jit(solution)/shard_map/while/body/eval_jaxpr/scatter-add | solution.py:96
  161.6 3.6 broadcast_in_dim.55
  165.2 77.5 %while.40 = (s32[]{:T(128)}, f32[2,256,26,128]{3,1,2,0:T(8,128)}, s32[2,32]{1,0:T(2,128)S(1)}, bf16[2,32,3,128,128]{4,3,2,1,0:T(8,128)(2,1)}, s32[2,32]{1,0:T(2,...) while((s32[]{:T(128)}, f32[2,256,26,128]{3,1,2,0:T(8,128)}, s32[2,32]{1,0:T(2,128)S(1)}, ...), condition=%wide.region_2.4_spmd, body=%wide.region_0.3_spmd.sunk | while | flops 540017984 | bytes 59774484 | solution.py:24
  165.3 4.3 %gather_fusion = bf16[32,256,128]{2,1,0:T(8,128)(2,1)} fusion(bf16[256,64,128]{2,0,1:T(8,128)(2,1)} %get-tuple-element.487, s32[1024]{0:T(1024)S(1)} %pad_clamp_fusion.8), kind=kCustom, calls=%fused_computation.clone.clone.1 | custom fusion | bytes 4194432 | tf_op jit(solution)/shard_map/while/body/eval_jaxpr/jit(_take)/gather | solution.py:59
  169.6 6.8 %convolution_bitcast_fusion.2 = f32[32,2,256,128]{2,3,1,0:T(8,128)} fusion(bf16[2,32,3,128,128]{4,3,2,1,0:T(8,128)(2,1)} %get-tuple-element.485, s32[]{:T(128)} %get-tuple-element.475, bf16[32,256,128]{2,1,0:T(8,128)(2,1)} %gather_fusion, pred[32]{0:T(512)(128)(4,1)S(1)} %get-tuple-element.443), kind=kOutput, calls=%fused_computation.45.clone.1 | convolution fusion | flops 537919488 | bytes 13632032 | tf_op jit(solution)/shard_map/while/body/eval_jaxpr/tsa,sgab->gtsb/dot_general | solution.py:60
  176.4 9.0 %copy.102 = f32[32,2,256,128]{3,2,1,0:T(8,128)} copy(f32[32,2,256,128]{2,3,1,0:T(8,128)} %convolution_bitcast_fusion.2) | data formatting | bytes 16777216 | tf_op jit(solution)/shard_map/while/body/eval_jaxpr/tsa,sgab->gtsb/transpose | solution.py:60
  185.4 18.7 %scatter_fusion = f32[2,256,26,128]{3,1,2,0:T(8,128)} fusion(f32[2,256,26,128]{3,1,2,0:T(8,128)} %get-tuple-element.476, s32[32]{0:T(128)S(1)} %fusion.68, f32[32,2,256,128]{3,2,1,0:T(8,128)} %copy.102), kind=kCustom, calls=%fused_computation.4.clone.1 | custom fusion | flops 2097152 | bytes 25165952 | tf_op jit(solution)/shard_map/while/body/eval_jaxpr/scatter-add | solution.py:63
  204.1 4.3 %gather_fusion = bf16[32,256,128]{2,1,0:T(8,128)(2,1)} fusion(bf16[256,64,128]{2,0,1:T(8,128)(2,1)} %get-tuple-element.487, s32[1024]{0:T(1024)S(1)} %pad_clamp_fusion.8), kind=kCustom, calls=%fused_computation.clone.clone.1 | custom fusion | bytes 4194432 | tf_op jit(solution)/shard_map/while/body/eval_jaxpr/jit(_take)/gather | solution.py:59
  208.4 6.8 %convolution_bitcast_fusion.2 = f32[32,2,256,128]{2,3,1,0:T(8,128)} fusion(bf16[2,32,3,128,128]{4,3,2,1,0:T(8,128)(2,1)} %get-tuple-element.485, s32[]{:T(128)} %get-tuple-element.475, bf16[32,256,128]{2,1,0:T(8,128)(2,1)} %gather_fusion, pred[32]{0:T(512)(128)(4,1)S(1)} %get-tuple-element.443), kind=kOutput, calls=%fused_computation.45.clone.1 | convolution fusion | flops 537919488 | bytes 13632032 | tf_op jit(solution)/shard_map/while/body/eval_jaxpr/tsa,sgab->gtsb/dot_general | solution.py:60
  215.2 9.0 %copy.102 = f32[32,2,256,128]{3,2,1,0:T(8,128)} copy(f32[32,2,256,128]{2,3,1,0:T(8,128)} %convolution_bitcast_fusion.2) | data formatting | bytes 16777216 | tf_op jit(solution)/shard_map/while/body/eval_jaxpr/tsa,sgab->gtsb/transpose | solution.py:60
  224.2 18.6 %scatter_fusion = f32[2,256,26,128]{3,1,2,0:T(8,128)} fusion(f32[2,256,26,128]{3,1,2,0:T(8,128)} %get-tuple-element.476, s32[32]{0:T(128)S(1)} %fusion.68, f32[32,2,256,128]{3,2,1,0:T(8,128)} %copy.102), kind=kCustom, calls=%fused_computation.4.clone.1 | custom fusion | flops 2097152 | bytes 25165952 | tf_op jit(solution)/shard_map/while/body/eval_jaxpr/scatter-add | solution.py:63
  242.8 4.9 %fusion.51 = (bf16[1,256,26,128]{3,1,2,0:T(8,128)(2,1)S(1)}, bf16[1,256,26,128]{3,1,2,0:T(8,128)(2,1)S(1)}, bf16[256,26,128]{2,0,1:T(8,128)(2,1)}) fusion(f32[2,256,26,128]{3,1,2,0:T(8,128)} %get-tuple-element.131, f32[256,26,128]{2,0,1:T(8,128)S(1)} %get-tuple-element.133), kind=kLoop, calls=%fused_computation.101 | loop fusion | flops 12779520 | bytes 15335424 | tf_op jit(solution)/shard_map/stack | solution.py:105
  248.0 4.3 %broadcast.152.clone.1 = f32[256,64,128]{2,0,1:T(8,128)} broadcast(f32[]{:T(128)} %constant.109.clone.1), dimensions={} | broadcast | bytes 8388612 | tf_op jit(solution)/shard_map/broadcast.20
  252.3 39.0 %while.43 = (s32[]{:T(128)}, f32[256,64,128]{2,0,1:T(8,128)}, s32[2,32]{1,0:T(2,128)S(1)}, bf16[2,32,3,128,128]{4,3,2,1,0:T(8,128)(2,1)}, s32[2,32]{1,0:T(2,128)...) while((s32[]{:T(128)}, f32[256,64,128]{2,0,1:T(8,128)}, s32[2,32]{1,0:T(2,128)S(1)}, ...), condition=%wide.region_12.14_spmd, body=%wide.region_10.13_spmd.sunk | while | flops 540018048 | bytes 54531732 | solution.py:24
  252.3 3.0 gather_fusion.3
  258.5 3.2 fusion.78
  261.7 10.1 %scatter_fusion.3 = f32[256,64,128]{2,0,1:T(8,128)} fusion(f32[256,64,128]{2,0,1:T(8,128)} %get-tuple-element.539, s32[32]{0:T(128)S(1)} %get-tuple-element.466, f32[32,256,128]{2,1,0:T(8,128)} %fusion.78), kind=kCustom, calls=%fused_computation.6.clone.1 | custom fusion | flops 1048576 | bytes 12583040 | tf_op jit(solution)/shard_map/while/body/eval_jaxpr/scatter-add | solution.py:113
  271.8 3.0 gather_fusion.3
  278.0 3.3 fusion.78
  281.3 10.0 %scatter_fusion.3 = f32[256,64,128]{2,0,1:T(8,128)} fusion(f32[256,64,128]{2,0,1:T(8,128)} %get-tuple-element.539, s32[32]{0:T(128)S(1)} %get-tuple-element.466, f32[32,256,128]{2,1,0:T(8,128)} %fusion.78), kind=kCustom, calls=%fused_computation.6.clone.1 | custom fusion | flops 1048576 | bytes 12583040 | tf_op jit(solution)/shard_map/while/body/eval_jaxpr/scatter-add | solution.py:113
  291.3 6.0 %copy_bitcast_fusion = bf16[256,8192]{1,0:T(8,128)(2,1)} fusion(f32[256,64,128]{2,0,1:T(8,128)} %get-tuple-element.134), kind=kLoop, calls=%fused_computation.81 | loop fusion | flops 2097152 | bytes 12582912 | tf_op jit(solution)/shard_map/convert_element_type | solution.py:119
  297.5 4.3 %broadcast.152.clone = f32[256,64,128]{2,0,1:T(8,128)} broadcast(f32[]{:T(128)} %constant.109.clone.1), dimensions={} | broadcast | bytes 8388612 | tf_op jit(solution)/shard_map/broadcast.20
  301.8 35.5 %while.41 = (s32[]{:T(128)}, f32[256,64,128]{2,0,1:T(8,128)}, s32[2,32]{1,0:T(2,128)S(1)}, bf16[2,32,3,128,128]{4,3,1,2,0:T(8,128)(2,1)}, s32[2,32]{1,0:T(2,128)S(1)}, /*index=5*/bf16[256,26,128]{2,0,1:T(8,128)(2,1)}, s32[]{:T(128)}) while((s32[]{:T(128)}, f32[256,64,128]{2,0,1:T(8,128)}, s32[2,32]{1,0:T(2,128)S(1)}, ...), condition=%wide.region_5.7_spmd, body=%wide.region_3.6_spmd.sunk | while | flops 270534016 | bytes 30414456 | solution.py:24
  306.7 2.7 fusion.71
  309.4 10.2 %scatter_fusion.1 = f32[256,64,128]{2,0,1:T(8,128)} fusion(f32[256,64,128]{2,0,1:T(8,128)} %get-tuple-element.518, s32[32]{0:T(128)S(1)} %get-tuple-element.450, f32[32,256,128]{2,1,0:T(8,128)} %fusion.71), kind=kCustom, calls=%fused_computation.5.clone.1 | custom fusion | flops 1048576 | bytes 12583040 | tf_op jit(solution)/shard_map/while/body/eval_jaxpr/scatter-add | solution.py:80
  324.4 2.7 fusion.71
  327.1 10.1 %scatter_fusion.1 = f32[256,64,128]{2,0,1:T(8,128)} fusion(f32[256,64,128]{2,0,1:T(8,128)} %get-tuple-element.518, s32[32]{0:T(128)S(1)} %get-tuple-element.450, f32[32,256,128]{2,1,0:T(8,128)} %fusion.71), kind=kCustom, calls=%fused_computation.5.clone.1 | custom fusion | flops 1048576 | bytes 12583040 | tf_op jit(solution)/shard_map/while/body/eval_jaxpr/scatter-add | solution.py:80
  337.2 6.1 %copy_bitcast_fusion.1 = bf16[256,8192]{1,0:T(8,128)(2,1)} fusion(f32[256,64,128]{2,0,1:T(8,128)} %get-tuple-element.132), kind=kLoop, calls=%fused_computation.82 | loop fusion | flops 2097152 | bytes 12582912 | tf_op jit(solution)/shard_map/convert_element_type | solution.py:86
  343.3 3.9 reduce-scatter.5.cloned.1.call-done
  347.2 51.0 %reduce-scatter.3.cloned.1.call-done = bf16[256,1024]{1,0:T(8,128)(2,1)} async-done(((bf16[256,8192]{1,0:T(8,128)(2,1)}), bf16[256,1024]{1,0:T(8,128)(2,1)}) %reduce-scatter.3.cloned.1.call-update) | async-done | bytes 524304 | tf_op jit(solution)/shard_map/reduce_scatter | solution.py:85
  (76 shorter events, 25.4 us)
Async XLA Ops:
  7.2 44.4 %copy-start.4 = (s32[8]{0:T(128)S(1)}, s32[8]{0:T(128)}, u32[]{:S(2)}) copy-start(s32[8]{0:T(128)} %param.19) | copy-start | bytes 100
  7.2 48.4 %copy-start.3 = (s32[8,2]{0,1:T(2,128)S(1)}, s32[8,2]{0,1:T(2,128)}, u32[]{:S(2)}) copy-start(s32[8,2]{0,1:T(2,128)} %param.18) | copy-start | bytes 196
  7.2 113.8 %all-gather.4.cloned.1.call-start = ((), (), s32[]{:S(2)}) async-start(), calls=%async_computation.5 | async-start | bytes 7864320 | tf_op jit(solution)/shard_map/all_gather | solution.py:42
  52.2 31.2 %all-to-all-start.1 = ((s32[8,1,1]{2,1,0:T(1,128)}), s32[8,1,1]{2,1,0:T(1,128)S(1)}, u32[]{:S(2)}, u32[]{:S(2)}) async-start(s32[8,1,1]{2,1,0:T(1,128)} %copy.83), calls=%async_computation.1 | async-start | bytes 8192 | tf_op jit(solution)/shard_map/all_to_all | solution.py:39
  75.8 6.4 %copy-start.5 = (u32[32]{0:T(128)S(1)}, u32[32]{0:T(128)}, u32[]{:S(2)}) copy-start(u32[32]{0:T(128)} %constant.120) | copy-start | bytes 388
  83.4 13.3 %all-to-all-start = ((s32[8,1,2]{2,1,0:T(1,128)}), s32[8,1,2]{2,1,0:T(1,128)S(1)}, u32[]{:S(2)}, u32[]{:S(2)}) async-start(s32[8,1,2]{2,1,0:T(1,128)} %copy.78), calls=%async_computation | async-start | bytes 8192 | tf_op jit(solution)/shard_map/all_to_all | solution.py:38
  88.4 258.8 %reduce-scatter.5.cloned.1.call-start = ((), (), s32[]{:S(2)}) async-start(), calls=%async_computation.7 | async-start | bytes 4718592 | tf_op jit(solution)/shard_map/reduce_scatter | solution.py:118
  124.3 4.5 %copy-start = (bf16[2,32,3,128,128]{4,3,2,1,0:T(8,128)(2,1)}, bf16[2,32,3,128,128]{4,3,2,1,0:T(8,128)(2,1)S(1)}, u32[]{:S(2)}) copy-start(bf16[2,32,3,128,128]{4,3,2,1,0:T(8,128)(2,1)S(1)} %bitcast_select_fusion) | copy-start | bytes 18874372
  133.7 2.5 copy-start.1
  149.9 2.5 copy-start.1
  255.3 3.1 copy-start.2
  274.9 3.1 copy-start.2
  297.2 101.0 %reduce-scatter.3.cloned.1.call-start = ((), (), s32[]{:S(2)}) async-start(), calls=%async_computation.6 | async-start | bytes 4718592 | tf_op jit(solution)/shard_map/reduce_scatter | solution.py:85
Sparse Core Ops, SparseCore 0:
  51.6 69.3 all-gather.3
  297.4 49.7 reduce-scatter.4
  350.0 48.1 reduce-scatter.2
where the time goes:
time: 407 us; the launch traced here: 405 us
  other arithmetic  112 us (28%)
  local copies, waits for them, and re-layouts  108 us (27%)
  waiting for transfers between devices  70.5 us (17%)
  blocking collectives  60.1 us (15%)
  matrix products  30.9 us (8%)
  between operations  14.5 us (4%)
  starting transfers between devices  8.66 us (2%)
    reduce_scatter x1, waiting for transfers between devices, body(): lax.psum_scatter(out_part.astype(jnp.bfloat16), 'tensor', scatter_dimensi...  51 us
    all_to_all x1, blocking collectives, body(): lax.all_to_all(weight_tiles, 'tensor', split_axis=0, concat_axis=0, tiled...  44.3 us
    scatter-add x2, other arithmetic, gate_up_step(): return acc_value.at[:, :, col_block, :].add(products)  37.3 us
    scatter-add x2, other arithmetic, down_step(): return acc_value.at[:, row_block, :].add(products)  20.3 us
    scatter-add x2, other arithmetic, input_step(): return acc_value.at[:, row_block, :].add(products)  20.1 us
    transpose x2, local copies, waits for them, and re-layouts, gate_up_step(): jnp.einsum('tsa,sgab->gtsb', gathered, weights[:, 0:2], preferred_element...  17.9 us
    while x3, local copies, waits for them, and re-layouts, over_blocks(): running, _ = lax.scan(advance, running, shaped)  17.3 us
    all_gather x1, waiting for transfers between devices, body(): lax.all_gather(arrived_tiles, 'dp', axis=0, tiled=True)  15.5 us
  transfers between devices with their start and end apart: 5, of which 3 were waited for; matrix products, arithmetic and copies ran while one was open for 18% of the time, Pallas kernels for 0%

commit v1 on v0

--- a/solution.py
+++ b/solution.py
@@ -4,6 +4,27 @@
 from jax.sharding import PartitionSpec as P
 
 FF = 26624
+
+
+def collect(x, axis, dim):
+    devices, index, rows = (lax.axis_size(axis), lax.axis_index(axis), x.shape[dim])
+    right = [(i, (i + 1) % devices) for i in range(devices)]
+    left = [(i, (i - 1) % devices) for i in range(devices)]
+    filled = jnp.zeros((*x.shape[:dim], devices * rows, *x.shape[dim + 1 :]), x.dtype)
+    filled = lax.dynamic_update_slice_in_dim(filled, x, index * rows, axis=dim)
+    from_left = from_right = x
+    half = devices // 2
+    for turn in range(1, half + 1):
+        from_left = lax.ppermute(from_left, axis, right)
+        filled = lax.dynamic_update_slice_in_dim(
+            filled, from_left, (index - turn) % devices * rows, axis=dim
+        )
+        if turn < devices - half:
+            from_right = lax.ppermute(from_right, axis, left)
+            filled = lax.dynamic_update_slice_in_dim(
+                filled, from_right, (index + turn) % devices * rows, axis=dim
+            )
+    return filled
 
 
 def block_length(extent):
@@ -39,7 +60,7 @@
         lax.all_to_all(live_counts, "tensor", split_axis=0, concat_axis=0, tiled=True),
     )
     slot_tiles, slot_places, slot_counts = (
-        lax.all_gather(arrived_tiles, "dp", axis=0, tiled=True),
+        collect(arrived_tiles, "dp", 0),
         lax.all_gather(arrived_places, "dp", axis=0, tiled=True),
         lax.all_gather(arrived_counts, "dp", axis=0, tiled=True),
     )

time: 407 us -> 450 us (1.11)
  blocking collectives: 60.1 us -> 81.5 us
  waiting for transfers between devices: 70.5 us -> 89 us
    ppermute x0 -> x3, waiting for transfers between devices: none -> 35.3 us  [the longest x2 35.3 us: collect(): from_left = lax.ppermute(from_left, axis, right)]
    unnamed x1, blocking collectives: 7.47 us -> 29 us
    all_gather x1 -> x0, waiting for transfers between devices: 15.5 us -> none  [body(): lax.all_gather(arrived_tiles, 'dp', axis=0, tiled=True)]
    unnamed x13 -> x9, local copies, waits for them, and re-layouts: 13.9 us -> 13.6 us
  transfers between devices with their start and end apart: 5 -> 7, of which waited for: 3 -> 3; matrix products, arithmetic and copies ran while one was open for 18% -> 18% of each run, Pallas kernels for 0% -> 0%
where the time goes in v1:
time: 450 us; the launch traced here: 448 us
  local copies, waits for them, and re-layouts  112 us (25%)
  other arithmetic  109 us (24%)
  waiting for transfers between devices  89 us (20%)
  blocking collectives  81.5 us (18%)
  matrix products  29.6 us (7%)
  between operations  14.9 us (3%)
  starting transfers between devices  12.1 us (3%)
    reduce_scatter x1, waiting for transfers between devices, body(): lax.psum_scatter(out_part.astype(jnp.bfloat16), 'tensor', scatter_dimensi...  51 us
    all_to_all x1, blocking collectives, body(): lax.all_to_all(weight_tiles, 'tensor', split_axis=0, concat_axis=0, tiled...  44.2 us
    scatter-add x2, other arithmetic, gate_up_step(): return acc_value.at[:, :, col_block, :].add(products)  37.4 us
    ppermute x2, waiting for transfers between devices, collect(): from_left = lax.ppermute(from_left, axis, right)  35.3 us
    unnamed x1, blocking collectives  29 us
    scatter-add x2, other arithmetic, down_step(): return acc_value.at[:, row_block, :].add(products)  20.3 us
    scatter-add x2, other arithmetic, input_step(): return acc_value.at[:, row_block, :].add(products)  20.1 us
    transpose x2, local copies, waits for them, and re-layouts, gate_up_step(): jnp.einsum('tsa,sgab->gtsb', gathered, weights[:, 0:2], preferred_element...  18 us
  transfers between devices with their start and end apart: 7, of which 3 were waited for; matrix products, arithmetic and copies ran while one was open for 18% of the time, Pallas kernels for 0%

profile of v1, /device:TPU:0, one launch (start us, length us, event | category | flops | bytes accessed | tf_op | source)
XLA Modules:
  0.0 448.2 jit_solution(2740299524343198)
XLA Ops:
  7.2 44.2 %all_to_all.29 = bf16[8,2,3,128,128]{4,3,2,1,0:T(8,128)(2,1)S(1)} all-to-all(bf16[8,2,3,128,128]{4,3,2,1,0:T(8,128)(2,1)} %param.17), channel_id=1, replica_groups=mesh['dp'=4,'tensor'=8] {'tensor'}, dimensions={0} | all-to-all | bytes 3145728 | tf_op jit(solution)/shard_map/all_to_all | solution.py:58
  54.3 35.3 %collective-permute-done = bf16[8,2,3,128,128]{4,3,2,1,0:T(8,128)(2,1)S(1)} collective-permute-done((bf16[8,2,3,128,128]{4,3,2,1,0:T(8,128)(2,1)S(1)}, bf16[8,2,3,128,128]{4,3,2,1,0:T(8,128)(2,1)S(1)}, u32[]{:S(2)}, u32[]{:S(2)}) %collective-permute-start) | collective-permute-done | bytes 1572896 | tf_op jit(solution)/shard_map/ppermute | solution.py:18
  91.5 3.3 all-to-all-start.1
  96.3 6.4 %copy.85 = bf16[256,8192]{0,1:T(8,128)(2,1)} copy(bf16[256,8192]{1,0:T(8,128)(2,1)} %param.15) | data formatting | bytes 8388608 | tf_op args[0]
  102.7 6.4 %copy.87 = bf16[256,64,128]{2,0,1:T(8,128)(2,1)} copy(bf16[256,64,128]{0,2,1:T(8,128)(2,1)} %bitcast.210) | data formatting | bytes 8388608 | tf_op jit(solution)/shard_map/while | solution.py:45
  109.1 6.4 %copy.90 = bf16[256,8192]{0,1:T(8,128)(2,1)} copy(bf16[256,8192]{1,0:T(8,128)(2,1)} %param.16) | data formatting | bytes 8388608 | tf_op args[1]
  115.4 6.4 %copy.92 = bf16[256,64,128]{2,0,1:T(8,128)(2,1)} copy(bf16[256,64,128]{0,2,1:T(8,128)(2,1)} %bitcast.211) | data formatting | bytes 8388608 | tf_op jit(solution)/shard_map/while | solution.py:45
  123.1 5.0 %all-to-all-start = ((s32[8,1,2]{2,1,0:T(1,128)}), s32[8,1,2]{2,1,0:T(1,128)S(1)}, u32[]{:S(2)}, u32[]{:S(2)}) async-start(s32[8,1,2]{2,1,0:T(1,128)} %copy.78), calls=%async_computation | async-start | bytes 8192 | tf_op jit(solution)/shard_map/all_to_all | solution.py:59
  128.6 29.0 %all-reduce = s32[32]{0:T(128)S(1)} all-reduce(s32[32]{0:T(128)S(1)} %dynamic-update-slice), channel_id=3, replica_groups=mesh['dp'=4,'tensor'=8] {'dp'}, use_global_device_ids=true, to_apply=%add | all-reduce | flops 32 | bytes 256
  157.9 8.3 %all-gather = s32[32,1,2]{2,1,0:T(1,128)S(1)} all-gather(s32[8,1,2]{2,1,0:T(1,128)S(1)} %all-to-all-done), channel_id=2, replica_groups=mesh['dp'=4,'tensor'=8] {'dp'}, dimensions={0}, use_global_device_ids=true | all-gather | bytes 320 | tf_op jit(solution)/shard_map/all_gather | solution.py:64
  172.6 4.5 %copy.88 = bf16[2,32,3,128,128]{4,3,1,2,0:T(8,128)(2,1)} copy(bf16[2,32,3,128,128]{4,3,2,1,0:T(8,128)(2,1)S(1)} %bitcast_select_fusion) | data formatting | bytes 12582912 | tf_op jit(solution)/shard_map/while | solution.py:45
  177.1 3.6 broadcast_in_dim.59
  180.7 74.1 %while.40 = (s32[]{:T(128)}, f32[2,256,26,128]{3,1,2,0:T(8,128)}, s32[2,32]{1,0:T(2,128)S(1)}, bf16[2,32,3,128,128]{4,3,2,1,0:T(8,128)(2,1)}, s32[2,32]{1,0:T(2,...) while((s32[]{:T(128)}, f32[2,256,26,128]{3,1,2,0:T(8,128)}, s32[2,32]{1,0:T(2,128)S(1)}, ...), condition=%wide.region_2.4_spmd, body=%wide.region_0.3_spmd.sunk | while | flops 540017984 | bytes 59774484 | solution.py:45
  180.7 3.1 gather_fusion
  183.9 6.2 %convolution_bitcast_fusion.2 = f32[32,2,256,128]{2,3,1,0:T(8,128)} fusion(bf16[2,32,3,128,128]{4,3,2,1,0:T(8,128)(2,1)} %get-tuple-element.485, s32[]{:T(128)} %get-tuple-element.475, bf16[32,256,128]{2,1,0:T(8,128)(2,1)S(1)} %gather_fusion, pred[32]{0:T(512)(128)(4,1)S(1)} %get-tuple-element.443), kind=kOutput, calls=%fused_computation.45.clone.1 | convolution fusion | flops 537919488 | bytes 13632032 | tf_op jit(solution)/shard_map/while/body/eval_jaxpr/tsa,sgab->gtsb/dot_general | solution.py:81
  190.0 9.0 %copy.102 = f32[32,2,256,128]{3,2,1,0:T(8,128)} copy(f32[32,2,256,128]{2,3,1,0:T(8,128)} %convolution_bitcast_fusion.2) | data formatting | bytes 16777216 | tf_op jit(solution)/shard_map/while/body/eval_jaxpr/tsa,sgab->gtsb/transpose | solution.py:81
  199.0 18.7 %scatter_fusion = f32[2,256,26,128]{3,1,2,0:T(8,128)} fusion(f32[2,256,26,128]{3,1,2,0:T(8,128)} %get-tuple-element.476, s32[32]{0:T(128)S(1)} %fusion.68, f32[32,2,256,128]{3,2,1,0:T(8,128)} %copy.102), kind=kCustom, calls=%fused_computation.4.clone.1 | custom fusion | flops 2097152 | bytes 25165952 | tf_op jit(solution)/shard_map/while/body/eval_jaxpr/scatter-add | solution.py:84
  217.8 3.1 gather_fusion
  221.0 6.2 %convolution_bitcast_fusion.2 = f32[32,2,256,128]{2,3,1,0:T(8,128)} fusion(bf16[2,32,3,128,128]{4,3,2,1,0:T(8,128)(2,1)} %get-tuple-element.485, s32[]{:T(128)} %get-tuple-element.475, bf16[32,256,128]{2,1,0:T(8,128)(2,1)S(1)} %gather_fusion, pred[32]{0:T(512)(128)(4,1)S(1)} %get-tuple-element.443), kind=kOutput, calls=%fused_computation.45.clone.1 | convolution fusion | flops 537919488 | bytes 13632032 | tf_op jit(solution)/shard_map/while/body/eval_jaxpr/tsa,sgab->gtsb/dot_general | solution.py:81
  227.1 9.0 %copy.102 = f32[32,2,256,128]{3,2,1,0:T(8,128)} copy(f32[32,2,256,128]{2,3,1,0:T(8,128)} %convolution_bitcast_fusion.2) | data formatting | bytes 16777216 | tf_op jit(solution)/shard_map/while/body/eval_jaxpr/tsa,sgab->gtsb/transpose | solution.py:81
  236.1 18.6 %scatter_fusion = f32[2,256,26,128]{3,1,2,0:T(8,128)} fusion(f32[2,256,26,128]{3,1,2,0:T(8,128)} %get-tuple-element.476, s32[32]{0:T(128)S(1)} %fusion.68, f32[32,2,256,128]{3,2,1,0:T(8,128)} %copy.102), kind=kCustom, calls=%fused_computation.4.clone.1 | custom fusion | flops 2097152 | bytes 25165952 | tf_op jit(solution)/shard_map/while/body/eval_jaxpr/scatter-add | solution.py:84
  255.1 32.3 %while.42 = (s32[]{:T(128)}, f32[256,26,128]{2,0,1:T(8,128)S(1)}, s32[2,32]{1,0:T(2,128)S(1)}, bf16[2,32,3,128,128]{4,3,1,2,0:T(8,128)(2,1)}, s32[2,32]{1,0:T(2,...) while((s32[]{:T(128)}, f32[256,26,128]{2,0,1:T(8,128)S(1)}, s32[2,32]{1,0:T(2,128)S(1)}, ...), condition=%wide.region_9.11_spmd, body=%wide.region_7.10_spmd.sunk | while | flops 270533920 | bytes 38802964 | solution.py:45
  255.2 4.3 gather_fusion.2
  259.5 2.4 dynamic-slice_bitcast_fusion.7
  262.0 2.7 fusion.74
  264.8 6.5 %scatter_fusion.2 = f32[256,26,128]{2,0,1:T(8,128)S(1)} fusion(f32[256,26,128]{2,0,1:T(8,128)S(1)} %get-tuple-element.497, s32[32]{0:T(128)S(1)} %fusion.73, f32[32,256,128]{2,1,0:T(8,128)} %fusion.74), kind=kCustom, calls=%fused_computation.7.clone.1 | custom fusion | flops 1048576 | bytes 12583040 | tf_op jit(solution)/shard_map/while/body/eval_jaxpr/scatter-add | solution.py:117
  271.3 4.3 gather_fusion.2
  278.2 2.7 fusion.74
  280.9 6.5 %scatter_fusion.2 = f32[256,26,128]{2,0,1:T(8,128)S(1)} fusion(f32[256,26,128]{2,0,1:T(8,128)S(1)} %get-tuple-element.497, s32[32]{0:T(128)S(1)} %fusion.73, f32[32,256,128]{2,1,0:T(8,128)} %fusion.74), kind=kCustom, calls=%fused_computation.7.clone.1 | custom fusion | flops 1048576 | bytes 12583040 | tf_op jit(solution)/shard_map/while/body/eval_jaxpr/scatter-add | solution.py:117
  287.4 4.9 %fusion.51 = (bf16[1,256,26,128]{3,1,2,0:T(8,128)(2,1)S(1)}, bf16[1,256,26,128]{3,1,2,0:T(8,128)(2,1)S(1)}, bf16[256,26,128]{2,0,1:T(8,128)(2,1)}) fusion(f32[2,256,26,128]{3,1,2,0:T(8,128)} %get-tuple-element.131, f32[256,26,128]{2,0,1:T(8,128)S(1)} %get-tuple-element.133), kind=kLoop, calls=%fused_computation.101 | loop fusion | flops 12779520 | bytes 15335424 | tf_op jit(solution)/shard_map/stack | solution.py:126
  292.7 4.3 broadcast.157.clone.1
  296.9 38.9 %while.43 = (s32[]{:T(128)}, f32[256,64,128]{2,0,1:T(8,128)}, s32[2,32]{1,0:T(2,128)S(1)}, bf16[2,32,3,128,128]{4,3,2,1,0:T(8,128)(2,1)}, s32[2,32]{1,0:T(2,128)...) while((s32[]{:T(128)}, f32[256,64,128]{2,0,1:T(8,128)}, s32[2,32]{1,0:T(2,128)S(1)}, ...), condition=%wide.region_12.14_spmd, body=%wide.region_10.13_spmd.sunk | while | flops 540018048 | bytes 54531732 | solution.py:45
  296.9 3.0 gather_fusion.3
  303.1 3.2 fusion.78
  306.3 10.1 %scatter_fusion.3 = f32[256,64,128]{2,0,1:T(8,128)} fusion(f32[256,64,128]{2,0,1:T(8,128)} %get-tuple-element.539, s32[32]{0:T(128)S(1)} %get-tuple-element.466, f32[32,256,128]{2,1,0:T(8,128)} %fusion.78), kind=kCustom, calls=%fused_computation.6.clone.1 | custom fusion | flops 1048576 | bytes 12583040 | tf_op jit(solution)/shard_map/while/body/eval_jaxpr/scatter-add | solution.py:134
  316.4 3.0 gather_fusion.3
  322.6 3.2 fusion.78
  325.8 10.0 %scatter_fusion.3 = f32[256,64,128]{2,0,1:T(8,128)} fusion(f32[256,64,128]{2,0,1:T(8,128)} %get-tuple-element.539, s32[32]{0:T(128)S(1)} %get-tuple-element.466, f32[32,256,128]{2,1,0:T(8,128)} %fusion.78), kind=kCustom, calls=%fused_computation.6.clone.1 | custom fusion | flops 1048576 | bytes 12583040 | tf_op jit(solution)/shard_map/while/body/eval_jaxpr/scatter-add | solution.py:134
  335.9 6.0 %copy_bitcast_fusion = bf16[256,8192]{1,0:T(8,128)(2,1)} fusion(f32[256,64,128]{2,0,1:T(8,128)} %get-tuple-element.134), kind=kLoop, calls=%fused_computation.81 | loop fusion | flops 2097152 | bytes 12582912 | tf_op jit(solution)/shard_map/convert_element_type | solution.py:140
  342.1 4.3 broadcast.157.clone
  346.4 35.3 %while.41 = (s32[]{:T(128)}, f32[256,64,128]{2,0,1:T(8,128)}, s32[2,32]{1,0:T(2,128)S(1)}, bf16[2,32,3,128,128]{4,3,1,2,0:T(8,128)(2,1)}, s32[2,32]{1,0:T(2,128)S(1)}, /*index=5*/bf16[256,26,128]{2,0,1:T(8,128)(2,1)}, s32[]{:T(128)}) while((s32[]{:T(128)}, f32[256,64,128]{2,0,1:T(8,128)}, s32[2,32]{1,0:T(2,128)S(1)}, ...), condition=%wide.region_5.7_spmd, body=%wide.region_3.6_spmd.sunk | while | flops 270534016 | bytes 30414456 | solution.py:45
  351.2 2.7 fusion.71
  353.9 10.2 %scatter_fusion.1 = f32[256,64,128]{2,0,1:T(8,128)} fusion(f32[256,64,128]{2,0,1:T(8,128)} %get-tuple-element.518, s32[32]{0:T(128)S(1)} %get-tuple-element.450, f32[32,256,128]{2,1,0:T(8,128)} %fusion.71), kind=kCustom, calls=%fused_computation.5.clone.1 | custom fusion | flops 1048576 | bytes 12583040 | tf_op jit(solution)/shard_map/while/body/eval_jaxpr/scatter-add | solution.py:101
  368.8 2.7 fusion.71
  371.5 10.1 %scatter_fusion.1 = f32[256,64,128]{2,0,1:T(8,128)} fusion(f32[256,64,128]{2,0,1:T(8,128)} %get-tuple-element.518, s32[32]{0:T(128)S(1)} %get-tuple-element.450, f32[32,256,128]{2,1,0:T(8,128)} %fusion.71), kind=kCustom, calls=%fused_computation.5.clone.1 | custom fusion | flops 1048576 | bytes 12583040 | tf_op jit(solution)/shard_map/while/body/eval_jaxpr/scatter-add | solution.py:101
  381.7 6.0 %copy_bitcast_fusion.1 = bf16[256,8192]{1,0:T(8,128)(2,1)} fusion(f32[256,64,128]{2,0,1:T(8,128)} %get-tuple-element.132), kind=kLoop, calls=%fused_computation.82 | loop fusion | flops 2097152 | bytes 12582912 | tf_op jit(solution)/shard_map/convert_element_type | solution.py:107
  387.7 2.6 reduce-scatter.5.cloned.1.call-done
  390.3 51.0 %reduce-scatter.3.cloned.1.call-done = bf16[256,1024]{1,0:T(8,128)(2,1)} async-done(((bf16[256,8192]{1,0:T(8,128)(2,1)}), bf16[256,1024]{1,0:T(8,128)(2,1)}) %reduce-scatter.3.cloned.1.call-update) | async-done | bytes 524304 | tf_op jit(solution)/shard_map/reduce_scatter | solution.py:106
  (80 shorter events, 33.5 us)
Async XLA Ops:
  51.3 38.2 %collective-permute-start = (bf16[8,2,3,128,128]{4,3,2,1,0:T(8,128)(2,1)S(1)}, bf16[8,2,3,128,128]{4,3,2,1,0:T(8,128)(2,1)S(1)}, u32[]{:S(2)}, u32[]{:S(2)}) collective-permute-start(bf16[8,2,3,128,128]{4,3,2,1,0:T(8,128)(2,1)S(1)} %all_to_all.29), channel_id=1, source_target_pairs={{0,8},{8,16},{16,24},{24,0},{1,9},{9,17},{17,25},{25,1},{2,10},{10... | collective-permute-start | bytes 4718600 | tf_op jit(solution)/shard_map/ppermute | solution.py:18
  52.8 115.9 %collective-permute-start.1 = (bf16[8,2,3,128,128]{4,3,2,1,0:T(8,128)(2,1)S(1)}, bf16[8,2,3,128,128]{4,3,2,1,0:T(8,128)(2,1)}, u32[]{:S(2)}, u32[]{:S(2)}) collective-permute-start(bf16[8,2,3,128,128]{4,3,2,1,0:T(8,128)(2,1)S(1)} %all_to_all.29), channel_id=1, source_target_pairs={{0,24},{8,0},{16,8},{24,16},{1,25},{9,1},{17,9},{25,17},{2,26},{10... | collective-permute-start | bytes 4718600 | tf_op jit(solution)/shard_map/ppermute | solution.py:23
  89.6 80.8 %collective-permute-start.2 = (bf16[8,2,3,128,128]{4,3,2,1,0:T(8,128)(2,1)S(1)}, bf16[8,2,3,128,128]{4,3,2,1,0:T(8,128)(2,1)}, u32[]{:S(2)}, u32[]{:S(2)}) collective-permute-start(bf16[8,2,3,128,128]{4,3,2,1,0:T(8,128)(2,1)S(1)} %collective-permute-done), channel_id=1, source_target_pairs={{0,8},{8,16},{16,24},{24,0},{1,9},{9,17},{17,25},{25,1},{2,10},{10... | collective-permute-start | bytes 4718600 | tf_op jit(solution)/shard_map/ppermute | solution.py:18
  91.5 31.6 %all-to-all-start.1 = ((s32[8,1,1]{2,1,0:T(1,128)}), s32[8,1,1]{2,1,0:T(1,128)S(1)}, u32[]{:S(2)}, u32[]{:S(2)}) async-start(s32[8,1,1]{2,1,0:T(1,128)} %copy.83), calls=%async_computation.1 | async-start | bytes 8192 | tf_op jit(solution)/shard_map/all_to_all | solution.py:60
  115.4 6.4 %copy-start.3 = (u32[32]{0:T(128)S(1)}, u32[32]{0:T(128)}, u32[]{:S(2)}) copy-start(u32[32]{0:T(128)} %constant.155) | copy-start | bytes 388
  123.1 34.8 %all-to-all-start = ((s32[8,1,2]{2,1,0:T(1,128)}), s32[8,1,2]{2,1,0:T(1,128)S(1)}, u32[]{:S(2)}, u32[]{:S(2)}) async-start(s32[8,1,2]{2,1,0:T(1,128)} %copy.78), calls=%async_computation | async-start | bytes 8192 | tf_op jit(solution)/shard_map/all_to_all | solution.py:59
  128.1 262.2 %reduce-scatter.5.cloned.1.call-start = ((), (), s32[]{:S(2)}) async-start(), calls=%async_computation.6 | async-start | bytes 4718592 | tf_op jit(solution)/shard_map/reduce_scatter | solution.py:139
  172.6 4.5 %copy-start = (bf16[2,32,3,128,128]{4,3,2,1,0:T(8,128)(2,1)}, bf16[2,32,3,128,128]{4,3,2,1,0:T(8,128)(2,1)S(1)}, u32[]{:S(2)}) copy-start(bf16[2,32,3,128,128]{4,3,2,1,0:T(8,128)(2,1)S(1)} %bitcast_select_fusion) | copy-start | bytes 18874372
  259.5 2.5 copy-start.1
  275.7 2.5 copy-start.1
  300.0 3.1 copy-start.2
  319.5 3.1 copy-start.2
  341.8 99.5 %reduce-scatter.3.cloned.1.call-start = ((), (), s32[]{:S(2)}) async-start(), calls=%async_computation.5 | async-start | bytes 4718592 | tf_op jit(solution)/shard_map/reduce_scatter | solution.py:106
Sparse Core Ops, SparseCore 0:
  342.0 48.2 reduce-scatter.4
  393.2 48.1 reduce-scatter.2
